TPU v7x, 32 devices: a whole 2x2x4 slice. The times are simulated.
32 devices in a mesh: group: 2 (over x), row: 16 (over z, y, core).
Axes of the slice: x: 2, y: 2, z: 4, core: 2. Of those that a mesh axis runs over, the one named last changes fastest.
Arguments:
- base_currents: bfloat16 [32768, 1024], P(('group', 'row')), parts along dimension 0, may hold values from -6 to 6
- term_rows: bfloat16 [8192, 1024], P(('group', 'row')), parts along dimension 0, may hold values from -12 to 12
- term_owner: int32 [8192, 1], P(('group', 'row')), parts along dimension 0, may hold values from 0 to 15; in each aligned block of 256 rows (0 to 255, 256 to 511, ...) at most 32 rows name the same one
- term_slot: int32 [8192, 1], P(('group', 'row')), parts along dimension 0, may hold values from 0 to 1023
- inductance: bfloat16 [64, 20, 256, 256], P('row'), may hold values from -0.078125 to 0.078125
- block_cols: int32 [64, 20], P('row'), may hold values from 0 to 63, as said below
Outputs:
- flux: bfloat16 [32768, 1024], P(('group', 'row')), parts along dimension 0
There are 2 independent parts, one for each index of `group`. A program takes and returns all parts, laid end to end along the dimension named above; an argument that names none is the same for every part. Nothing has to cross between parts.
Inputs may be any that keep to these rules, and one draw needn't show every extreme that they name: `block_cols`: the block rows of device i (block rows i * 4 to i * 4 + 3) list only block columns of devices i - 2 to i + 2; every block row lists a column of device max(i - 2, 0) and one of device min(i + 2, the last device). Columns may repeat. `term_owner`: among the 256 terminal rows of one device, at most 32 name the same owner, and that many is reached.
All inputs are finite; a program needn't handle non-finite values.
Results may differ from a plain program's by a relative error of at most 0.0046.
Values may be sent and summed in bfloat16 or wider, within the bound.
A program may use at most 128 MiB of HBM per device.

v0:
```python
import functools

import jax
import jax.numpy as jnp
from jax import lax
from jax.experimental import pallas as pl
from jax.experimental.pallas import tpu as pltpu
from jax.sharding import PartitionSpec as P

CHUNKS = 4
LANES = 128
HALO = 2
MESH = pl.DeviceIdType.MESH
F32 = jnp.float32
BF16 = jnp.bfloat16
TO_Y, TO_Z, TO_CORE, TO_RELAY = range(4)


def kernel(n, cap, cols_hbm, owner_hbm, slot_hbm, terms_hbm, base_hbm, blocks_hbm, out_hbm, *scratch):
    windows, scratch = scratch[:CHUNKS], scratch[CHUNKS:]
    outgoing, scratch = scratch[:CHUNKS], scratch[CHUNKS:]
    arrived, scratch = scratch[:CHUNKS], scratch[CHUNKS:]
    results, scratch = scratch[:CHUNKS], scratch[CHUNKS:]
    (cols_ref, owner_ref, slot_ref, terms, base, blocks, landing, tags_out, tags_in,
     load_sem, own_sem, store_sem, a2a_send, a2a_recv, tag_sem, halo_send, halo_recv, piece_recv) = scratch
    me = lax.axis_index("row")
    count = terms.shape[0]
    seg_dev = base.shape[0]
    rows_dev, stored, block, _ = blocks.shape
    wide = windows[0].shape[2]
    sign_c = 1 - 2 * (me % 2)
    sign_y = 1 - 2 * ((me // 2) % 2)
    z_to, z_from = me + 4 * sign_y, me - 4 * sign_y
    z_sends = jnp.logical_and(z_to >= 0, z_to < n)
    z_comes = jnp.logical_and(z_from >= 0, z_from < n)

    load_terms = pltpu.make_async_copy(terms_hbm, terms, load_sem.at[0])
    load_base = pltpu.make_async_copy(base_hbm, base, load_sem.at[1])
    load_blocks = pltpu.make_async_copy(blocks_hbm, blocks, load_sem.at[2])
    load_owner = pltpu.make_async_copy(owner_hbm, owner_ref, load_sem.at[3])
    load_slot = pltpu.make_async_copy(slot_hbm, slot_ref, load_sem.at[4])
    load_cols = pltpu.make_async_copy(cols_hbm, cols_ref, load_sem.at[5])
    for load in (load_owner, load_slot, load_terms, load_base, load_cols, load_blocks):
        load.start()

    barrier = pltpu.get_barrier_semaphore()

    @pl.loop(1, n)
    def _(step):
        pl.semaphore_signal(barrier, inc=1, device_id={"row": (me + step) % n}, device_id_type=MESH)

    load_owner.wait()
    owner = owner_ref[...]
    matches = (lax.broadcasted_iota(jnp.int32, (n, count), 0) == owner).astype(F32)
    before = lax.broadcasted_iota(jnp.int32, (count, count), 0) < lax.broadcasted_iota(jnp.int32, (count, count), 1)
    earlier = jnp.dot(matches.astype(BF16), before.astype(F32).astype(BF16), preferred_element_type=F32)
    order_in = jnp.sum(earlier * matches, axis=0, keepdims=True).astype(jnp.int32)
    position = owner * cap + order_in
    picker = (lax.broadcasted_iota(jnp.int32, (n * cap, count), 0) == position).astype(F32).astype(BF16)
    def tag_copy(peer, source):
        return pltpu.make_async_remote_copy(
            src_ref=tags_out.at[peer], dst_ref=tags_in.at[source], send_sem=tag_sem.at[0],
            recv_sem=tag_sem.at[1], device_id={"row": peer}, device_id_type=MESH)

    def row_copy(j, peer, source):
        return pltpu.make_async_remote_copy(
            src_ref=outgoing[j].at[peer], dst_ref=arrived[j].at[source], send_sem=a2a_send.at[j],
            recv_sem=a2a_recv.at[j], device_id={"row": peer}, device_id_type=MESH)

    def all_tags():
        others = pl.ds(0, n - 1)
        return pltpu.make_async_remote_copy(
            src_ref=tags_out.at[others], dst_ref=tags_in.at[others], send_sem=tag_sem.at[0],
            recv_sem=tag_sem.at[1], device_id={"row": (me + 1) % n}, device_id_type=MESH)

    def all_rows(j):
        others = pl.ds(0, n - 1)
        return pltpu.make_async_remote_copy(
            src_ref=outgoing[j].at[others], dst_ref=arrived[j].at[others], send_sem=a2a_send.at[j],
            recv_sem=a2a_recv.at[j], device_id={"row": (me + 1) % n}, device_id_type=MESH)

    own_tags = pltpu.make_async_copy(tags_out.at[me], tags_in.at[me], own_sem.at[CHUNKS])
    own_rows = [
        pltpu.make_async_copy(outgoing[j].at[me], arrived[j].at[me], own_sem.at[j]) for j in range(CHUNKS)
    ]

    def pack(j):
        sent = jnp.dot(picker, terms[:, j * wide:(j + 1) * wide], preferred_element_type=F32)
        outgoing[j][...] = sent.astype(BF16).reshape(outgoing[j].shape)

    def send_rows(j):
        @pl.loop(1, n)
        def _(step):
            row_copy(j, (me + step) % n, me).start()

        own_rows[j].start()

    load_terms.wait()
    pack(0)
    pl.semaphore_wait(barrier, n - 1)
    send_rows(0)
    per_row = LANES // cap
    lane_of = order_in + (me % per_row) * cap
    lanes = (lax.broadcasted_iota(jnp.int32, (LANES, count), 0) == lane_of).astype(F32).astype(BF16)
    load_slot.wait()
    tag = slot_ref[...] + 1
    high = (tag // 32).astype(F32)
    low = (tag % 32).astype(F32)
    over_rows = (((1,), (1,)), ((), ()))
    tags = 32.0 * lax.dot_general((matches * high).astype(BF16), lanes, over_rows, preferred_element_type=F32)
    tags = tags + lax.dot_general((matches * low).astype(BF16), lanes, over_rows, preferred_element_type=F32)
    tags = tags.astype(jnp.int32)
    for peer in range(n):
        tags_out[peer] = jnp.broadcast_to(tags[peer:peer + 1], tags_out.shape[1:])


    @pl.loop(1, n)
    def _(step):
        tag_copy((me + step) % n, me).start()

    own_tags.start()
    for j in range(1, CHUNKS):
        pack(j)
        send_rows(j)

    all_tags().wait_recv()
    own_tags.wait()
    packed = []
    for first in range(0, n, per_row):
        total = tags_in[first][0:1]
        for source in range(first + 1, min(first + per_row, n)):
            total = total + tags_in[source][0:1]
        packed.append(total)
    arrived_tags = jnp.concatenate(packed, axis=1) - 1
    tall = seg_dev // 4
    for part in range(4):
        seg_ids = lax.broadcasted_iota(jnp.int32, (tall, n * cap), 0) + part * tall
        landing[part * tall:(part + 1) * tall] = (seg_ids == arrived_tags).astype(F32).astype(BF16)
    load_base.wait()

    def halo_copy(kind, j, from_slot, to_slot, peer):
        return pltpu.make_async_remote_copy(
            src_ref=windows[j].at[pl.ds(rows_dev * from_slot, rows_dev)],
            dst_ref=windows[j].at[pl.ds(rows_dev * to_slot, rows_dev)],
            send_sem=halo_send.at[kind, j], recv_sem=halo_recv.at[kind, j],
            device_id={"row": peer}, device_id_type=MESH)

    def piece_copy(kind, p, from_slot, to_slot, peer):
        j, q = divmod(p, rows_dev)
        recv_sem = halo_recv.at[kind, j] if kind == TO_RELAY else piece_recv.at[kind, p]
        return pltpu.make_async_remote_copy(
            src_ref=windows[j].at[rows_dev * from_slot + q], dst_ref=windows[j].at[rows_dev * to_slot + q],
            send_sem=halo_send.at[kind, j], recv_sem=recv_sem, device_id={"row": peer}, device_id_type=MESH)

    y_way = (HALO, HALO - 2 * sign_y, me + 2 * sign_y)
    core_way = (HALO, HALO - sign_c, me + sign_c)
    z_way = (HALO + 2 * sign_y, HALO - 2 * sign_y, z_to)
    relay_way = (HALO + 2 * sign_c, HALO + sign_c, me + sign_c)
    relay_sends = jnp.logical_or(sign_y == sign_c, z_comes)
    relay_comes = jnp.logical_or(sign_y != sign_c, z_comes)
    first_block = (me - HALO) * rows_dev
    pieces = CHUNKS * rows_dev

    def own(j):
        all_rows(j).wait_recv()
        own_rows[j].wait()
        rows = arrived[j][...].reshape(n * cap, wide)
        for q in range(rows_dev):
            place = slice(q * block, (q + 1) * block)
            injected = jnp.dot(landing[place], rows, preferred_element_type=F32)
            before_it = base[place, j * wide:(j + 1) * wide].astype(F32)
            windows[j][HALO * rows_dev + q] = (before_it + injected).astype(BF16)
            piece_copy(TO_Y, j * rows_dev + q, *y_way).start()
        halo_copy(TO_CORE, j, *core_way).start()

    def y_arrives(p):
        slot = HALO + 2 * sign_y
        piece_copy(TO_Y, p, slot, slot, me + 2 * sign_y).wait_recv()

        @pl.when(z_sends)
        def _():
            piece_copy(TO_Z, p, *z_way).start()

        @pl.when(sign_y == sign_c)
        def _():
            piece_copy(TO_RELAY, p, *relay_way).start()

    def z_arrives(p):
        slot = HALO - 2 * sign_y

        @pl.when(z_comes)
        def _():
            piece_copy(TO_Z, p, slot, slot, me + 2 * sign_y).wait_recv()

        @pl.when(jnp.logical_and(z_comes, sign_y != sign_c))
        def _():
            piece_copy(TO_RELAY, p, *relay_way).start()

    def window_complete(j):
        halo_copy(TO_CORE, j, HALO + sign_c, HALO + sign_c, me + sign_c).wait_recv()

        @pl.when(relay_comes)
        def _():
            halo_copy(TO_RELAY, j, HALO - sign_c, HALO - sign_c, me + sign_c).wait_recv()

    def compute(j, r):
        total = jnp.zeros((block, wide), F32)
        for k in range(stored):
            place = jnp.clip(cols_ref[r, k] - first_block, 0, windows[j].shape[0] - 1)
            total = total + jnp.dot(blocks[r, k], windows[j][place], preferred_element_type=F32)
        results[j][r * block:(r + 1) * block] = total.astype(BF16)

    def store(j):
        return pltpu.make_async_copy(results[j], out_hbm.at[:, pl.ds(j * wide, wide)], store_sem.at[j])

    own(0)
    own(1)
    z_lag, lag = 2, rows_dev + 2
    for p in range(pieces + lag):
        if p < pieces:
            y_arrives(p)
            if p % rows_dev == 0 and p // rows_dev + 2 < CHUNKS:
                own(p // rows_dev + 2)
        if 0 <= p - z_lag < pieces:
            z_arrives(p - z_lag)
        if p == lag:
            load_cols.wait()
            load_blocks.wait()
            all_tags().wait_send()
            for j in range(CHUNKS):
                all_rows(j).wait_send()
        if p >= lag:
            j, r = divmod(p - lag, rows_dev)
            if r == 0:
                window_complete(j)
            compute(j, r)
            if r == rows_dev - 1:
                store(j).start()

    for j in range(CHUNKS):
        halo_copy(TO_Y, j, *y_way).wait_send()
        halo_copy(TO_CORE, j, *core_way).wait_send()

        @pl.when(z_sends)
        def _():
            halo_copy(TO_Z, j, *z_way).wait_send()

        @pl.when(relay_sends)
        def _():
            halo_copy(TO_RELAY, j, *relay_way).wait_send()

        store(j).wait()


def shards(base_currents, term_rows, term_owner, term_slot, inductance, block_cols):
    n = lax.axis_size("row")
    seg_dev, width = base_currents.shape
    count = term_rows.shape[0]
    rows_dev, stored, block, _ = inductance.shape
    cap = max(16, 2 * count // n)
    wide = width // CHUNKS
    span = (2 * HALO + 1) * rows_dev
    hbm = pl.BlockSpec(memory_space=pl.ANY)
    dma = pltpu.SemaphoreType.DMA
    return pl.pallas_call(
        functools.partial(kernel, n, cap),
        out_shape=jax.ShapeDtypeStruct((seg_dev, width), BF16),
        in_specs=[hbm] * 6,
        out_specs=hbm,
        scratch_shapes=(
            [pltpu.VMEM((span, block, wide), BF16)] * CHUNKS
            + [pltpu.VMEM((n, cap, wide), BF16)] * CHUNKS
            + [pltpu.VMEM((n, cap, wide), BF16)] * CHUNKS
            + [pltpu.VMEM((seg_dev, wide), BF16)] * CHUNKS
            + [
                pltpu.SMEM(block_cols.shape, jnp.int32),
                pltpu.VMEM((1, count), jnp.int32),
                pltpu.VMEM((1, count), jnp.int32),
                pltpu.VMEM((count, width), BF16),
                pltpu.VMEM((seg_dev, width), BF16),
                pltpu.VMEM(inductance.shape, BF16),
                pltpu.VMEM((seg_dev, n * cap), BF16),
                pltpu.VMEM((n, 8, LANES), jnp.int32),
                pltpu.VMEM((n, 8, LANES), jnp.int32),
                dma((6,)),
                dma((CHUNKS + 1,)),
                dma((CHUNKS,)),
                dma((CHUNKS,)),
                dma((CHUNKS,)),
                dma((2,)),
                dma((4, CHUNKS)),
                dma((4, CHUNKS)),
                dma((2, CHUNKS * rows_dev)),
            ]
        ),
        compiler_params=pltpu.CompilerParams(
            collective_id=0, has_side_effects=True, vmem_limit_bytes=60 * 2**20
        ),
        cost_estimate=pl.CostEstimate(
            flops=2 * rows_dev * stored * block * block * width,
            bytes_accessed=2 * (inductance.size + 2 * base_currents.size + term_rows.size),
            transcendentals=0,
        ),
    )(block_cols, term_owner.reshape(1, count), term_slot.reshape(1, count), term_rows, base_currents, inductance)


def solution(mesh):
    placed = (
        P(("group", "row"), None),
        P(("group", "row"), None),
        P(("group", "row"), None),
        P(("group", "row"), None),
        P("row", None, None, None),
        P("row", None),
    )
    return jax.shard_map(
        shards, mesh=mesh, in_specs=placed, out_specs=P(("group", "row"), None), check_vma=False
    )
```

profile of v0, /device:TPU:5, one launch (start us, length us, event | category | flops | bytes accessed | tf_op | source)
XLA Modules:
  0.0 82.2 jit_solution(16680132946076764218)
XLA Ops:
  0.0 79.1 %shard_map.64 = bf16[1024,1024]{1,0:T(8,128)(2,1)} custom-call(s32[4,20]{1,0:T(4,128)} %cols_hbm.1, s32[1,256]{1,0:T(1,128)} %bitcast.2, s32[1,256]{1,0:T(1,128)} %bitcast.3, bf16[256,1024]{1,0:T(8,128)(2,1)} %terms_hbm.1, bf16[1024,1024]{1,0:T(8,128)(2,1)} %base_hbm.1, bf16[4,20,256,256]{3,2,1,0:T(8,128)(2,1)} %blocks_hbm.1), custom_call_target="tpu_custom_call" | custom-call | flops 10737418240 | bytes 15204352 | tf_op jit(solution)/shard_map/pallas_call | solution.py:265
  79.1 3.1 %copy.8 = bf16[1024,1024]{1,0:T(8,128)(2,1)} copy(bf16[1024,1024]{1,0:T(8,128)(2,1)} %shard_map.64) | data formatting | bytes 4194304
where the time goes:
time: 83.1 us; the launch traced here: 82.2 us
  Pallas kernels  79.1 us (95%)
  local copies, waits for them, and re-layouts  3.08 us (4%)
    pallas_call x1, Pallas kernels, shards(): pl.pallas_call(functools.partial(kernel, n, cap), out_shape=jax.ShapeDtyp...  79.1 us
    unnamed x1, local copies, waits for them, and re-layouts  3.08 us

commit v1 on v0

--- a/solution.py
+++ b/solution.py
@@ -7,27 +7,32 @@
 from jax.experimental.pallas import tpu as pltpu
 from jax.sharding import PartitionSpec as P
 
-CHUNKS = 4
+WIDTHS = (1, 1, 2, 2, 2)
+CHUNKS = len(WIDTHS)
 LANES = 128
 HALO = 2
 MESH = pl.DeviceIdType.MESH
 F32 = jnp.float32
 BF16 = jnp.bfloat16
 TO_Y, TO_Z, TO_CORE, TO_RELAY = range(4)
-
-
-def kernel(n, cap, cols_hbm, owner_hbm, slot_hbm, terms_hbm, base_hbm, blocks_hbm, out_hbm, *scratch):
+RELAYED = (1, 2)
+AHEAD = 2
+
+
+def kernel(n, cap, cols_hbm, owner_hbm, slot_hbm, terms_hbm, base_hbm, blocks_hbm, out_ref, *scratch):
     windows, scratch = scratch[:CHUNKS], scratch[CHUNKS:]
     outgoing, scratch = scratch[:CHUNKS], scratch[CHUNKS:]
     arrived, scratch = scratch[:CHUNKS], scratch[CHUNKS:]
-    results, scratch = scratch[:CHUNKS], scratch[CHUNKS:]
+    passing, scratch = scratch[:CHUNKS], scratch[CHUNKS:]
     (cols_ref, owner_ref, slot_ref, terms, base, blocks, landing, tags_out, tags_in,
-     load_sem, own_sem, store_sem, a2a_send, a2a_recv, tag_sem, halo_send, halo_recv, piece_recv) = scratch
+     load_sem, own_sem, a2a_send, a2a_recv, pass_send, pass_recv, tag_sem, halo_send, halo_recv,
+     piece_recv) = scratch
     me = lax.axis_index("row")
     count = terms.shape[0]
     seg_dev = base.shape[0]
     rows_dev, stored, block, _ = blocks.shape
-    wide = windows[0].shape[2]
+    wides = [window.shape[2] for window in windows]
+    starts = [sum(wides[:j]) for j in range(CHUNKS)]
     sign_c = 1 - 2 * (me % 2)
     sign_y = 1 - 2 * ((me // 2) % 2)
     z_to, z_from = me + 4 * sign_y, me - 4 * sign_y
@@ -55,8 +60,12 @@
     before = lax.broadcasted_iota(jnp.int32, (count, count), 0) < lax.broadcasted_iota(jnp.int32, (count, count), 1)
     earlier = jnp.dot(matches.astype(BF16), before.astype(F32).astype(BF16), preferred_element_type=F32)
     order_in = jnp.sum(earlier * matches, axis=0, keepdims=True).astype(jnp.int32)
-    position = owner * cap + order_in
+    position = ((owner // 2) % 2 * (n // 2) + owner // 4 * 2 + owner % 2) * cap + order_in
     picker = (lax.broadcasted_iota(jnp.int32, (n * cap, count), 0) == position).astype(F32).astype(BF16)
+
+    def slot_of(device):
+        return (device // 2) % 2 * (n // 2) + device // 4 * 2 + device % 2
+
     def tag_copy(peer, source):
         return pltpu.make_async_remote_copy(
             src_ref=tags_out.at[peer], dst_ref=tags_in.at[source], send_sem=tag_sem.at[0],
@@ -64,7 +73,7 @@
 
     def row_copy(j, peer, source):
         return pltpu.make_async_remote_copy(
-            src_ref=outgoing[j].at[peer], dst_ref=arrived[j].at[source], send_sem=a2a_send.at[j],
+            src_ref=outgoing[j].at[slot_of(peer)], dst_ref=arrived[j].at[source], send_sem=a2a_send.at[j],
             recv_sem=a2a_recv.at[j], device_id={"row": peer}, device_id_type=MESH)
 
     def all_tags():
@@ -81,24 +90,71 @@
 
     own_tags = pltpu.make_async_copy(tags_out.at[me], tags_in.at[me], own_sem.at[CHUNKS])
     own_rows = [
-        pltpu.make_async_copy(outgoing[j].at[me], arrived[j].at[me], own_sem.at[j]) for j in range(CHUNKS)
+        pltpu.make_async_copy(outgoing[j].at[slot_of(me)], arrived[j].at[me], own_sem.at[j]) for j in range(CHUNKS)
     ]
 
     def pack(j):
-        sent = jnp.dot(picker, terms[:, j * wide:(j + 1) * wide], preferred_element_type=F32)
+        sent = jnp.dot(picker, terms[:, starts[j]:starts[j] + wides[j]], preferred_element_type=F32)
         outgoing[j][...] = sent.astype(BF16).reshape(outgoing[j].shape)
+
+    my_z, y_peer = me // 4, me + 2 * sign_y
+
+    def over_y(j, hop):
+        first = slot_of(me + 2 * sign_y + 4 * hop * sign_y - me % 2)
+        return pltpu.make_async_remote_copy(
+            src_ref=outgoing[j].at[pl.ds(first, 2)], dst_ref=passing[j].at[hop - 1], send_sem=a2a_send.at[j],
+            recv_sem=pass_recv.at[j, hop - 1], device_id={"row": y_peer}, device_id_type=MESH)
+
+    def over_z(j, hop, core):
+        return pltpu.make_async_remote_copy(
+            src_ref=passing[j].at[hop - 1, core], dst_ref=arrived[j].at[y_peer],
+            send_sem=pass_send.at[j, hop - 1], recv_sem=a2a_recv.at[j],
+            device_id={"row": me - me % 2 + core - 4 * hop * sign_y}, device_id_type=MESH)
+
+    def passed(j, hop):
+        return pltpu.make_async_remote_copy(
+            src_ref=passing[j].at[hop - 1], dst_ref=passing[j].at[hop - 1], send_sem=pass_send.at[j, hop - 1],
+            recv_sem=pass_recv.at[j, hop - 1], device_id={"row": y_peer}, device_id_type=MESH)
+
+    def goes_over(hop):
+        there = my_z + hop * sign_y
+        return jnp.logical_and(there >= 0, there < n // 4)
+
+    def comes_over(hop):
+        there = my_z - hop * sign_y
+        return jnp.logical_and(there >= 0, there < n // 4)
+
+    def pass_rows(j):
+        for hop in RELAYED:
+            @pl.when(comes_over(hop))
+            def _(hop=hop):
+                passed(j, hop).wait_recv()
+                for core in range(2):
+                    over_z(j, hop, core).start()
+
+    def send_over(j):
+        for hop in reversed(RELAYED):
+            @pl.when(goes_over(hop))
+            def _(hop=hop):
+                over_y(j, hop).start()
 
     def send_rows(j):
         @pl.loop(1, n)
         def _(step):
-            row_copy(j, (me + step) % n, me).start()
+            peer = (me + step) % n
+            hops = (peer // 4 - my_z) * sign_y
+            other_y = (peer // 2) % 2 != (me // 2) % 2
+            over = jnp.logical_and(other_y, jnp.logical_and(hops >= min(RELAYED, default=n), hops <= max(RELAYED, default=0)))
+
+            @pl.when(jnp.logical_not(over))
+            def _():
+                row_copy(j, peer, me).start()
 
         own_rows[j].start()
 
     load_terms.wait()
-    pack(0)
-    pl.semaphore_wait(barrier, n - 1)
-    send_rows(0)
+    for j in range(CHUNKS):
+        pack(j)
     per_row = LANES // cap
     lane_of = order_in + (me % per_row) * cap
     lanes = (lax.broadcasted_iota(jnp.int32, (LANES, count), 0) == lane_of).astype(F32).astype(BF16)
@@ -113,15 +169,18 @@
     for peer in range(n):
         tags_out[peer] = jnp.broadcast_to(tags[peer:peer + 1], tags_out.shape[1:])
 
+    pl.semaphore_wait(barrier, n - 1)
+    send_over(0)
+    send_rows(0)
 
     @pl.loop(1, n)
     def _(step):
         tag_copy((me + step) % n, me).start()
 
     own_tags.start()
+    pass_rows(0)
     for j in range(1, CHUNKS):
-        pack(j)
-        send_rows(j)
+        send_over(j)
 
     all_tags().wait_recv()
     own_tags.wait()
@@ -164,11 +223,14 @@
     def own(j):
         all_rows(j).wait_recv()
         own_rows[j].wait()
-        rows = arrived[j][...].reshape(n * cap, wide)
+        if j + 1 < CHUNKS:
+            send_rows(j + 1)
+            pass_rows(j + 1)
+        rows = arrived[j][...].reshape(n * cap, wides[j])
         for q in range(rows_dev):
             place = slice(q * block, (q + 1) * block)
             injected = jnp.dot(landing[place], rows, preferred_element_type=F32)
-            before_it = base[place, j * wide:(j + 1) * wide].astype(F32)
+            before_it = base[place, starts[j]:starts[j] + wides[j]].astype(F32)
             windows[j][HALO * rows_dev + q] = (before_it + injected).astype(BF16)
             piece_copy(TO_Y, j * rows_dev + q, *y_way).start()
         halo_copy(TO_CORE, j, *core_way).start()
@@ -204,40 +266,33 @@
             halo_copy(TO_RELAY, j, HALO - sign_c, HALO - sign_c, me + sign_c).wait_recv()
 
     def compute(j, r):
-        total = jnp.zeros((block, wide), F32)
+        total = jnp.zeros((block, wides[j]), F32)
         for k in range(stored):
             place = jnp.clip(cols_ref[r, k] - first_block, 0, windows[j].shape[0] - 1)
             total = total + jnp.dot(blocks[r, k], windows[j][place], preferred_element_type=F32)
-        results[j][r * block:(r + 1) * block] = total.astype(BF16)
-
-    def store(j):
-        return pltpu.make_async_copy(results[j], out_hbm.at[:, pl.ds(j * wide, wide)], store_sem.at[j])
+        out_ref[r * block:(r + 1) * block, starts[j]:starts[j] + wides[j]] = total.astype(BF16)
 
     own(0)
-    own(1)
     z_lag, lag = 2, rows_dev + 2
     for p in range(pieces + lag):
         if p < pieces:
             y_arrives(p)
-            if p % rows_dev == 0 and p // rows_dev + 2 < CHUNKS:
-                own(p // rows_dev + 2)
+            if p % rows_dev == rows_dev - 1 - AHEAD and p // rows_dev + 1 < CHUNKS:
+                own(p // rows_dev + 1)
         if 0 <= p - z_lag < pieces:
             z_arrives(p - z_lag)
         if p == lag:
             load_cols.wait()
             load_blocks.wait()
-            all_tags().wait_send()
-            for j in range(CHUNKS):
-                all_rows(j).wait_send()
         if p >= lag:
             j, r = divmod(p - lag, rows_dev)
             if r == 0:
                 window_complete(j)
             compute(j, r)
-            if r == rows_dev - 1:
-                store(j).start()
-
+
+    all_tags().wait_send()
     for j in range(CHUNKS):
+        all_rows(j).wait_send()
         halo_copy(TO_Y, j, *y_way).wait_send()
         halo_copy(TO_CORE, j, *core_way).wait_send()
 
@@ -249,7 +304,10 @@
         def _():
             halo_copy(TO_RELAY, j, *relay_way).wait_send()
 
-        store(j).wait()
+        for hop in RELAYED:
+            @pl.when(comes_over(hop))
+            def _(hop=hop):
+                passed(j, hop).wait_send()
 
 
 def shards(base_currents, term_rows, term_owner, term_slot, inductance, block_cols):
@@ -258,20 +316,20 @@
     count = term_rows.shape[0]
     rows_dev, stored, block, _ = inductance.shape
     cap = max(16, 2 * count // n)
-    wide = width // CHUNKS
+    wides = [width * part // sum(WIDTHS) for part in WIDTHS]
     span = (2 * HALO + 1) * rows_dev
-    hbm = pl.BlockSpec(memory_space=pl.ANY)
+    hbm = pl.BlockSpec(memory_space=pltpu.HBM)
     dma = pltpu.SemaphoreType.DMA
     return pl.pallas_call(
         functools.partial(kernel, n, cap),
-        out_shape=jax.ShapeDtypeStruct((seg_dev, width), BF16),
+        out_shape=pltpu.VMEM((seg_dev, width), BF16),
         in_specs=[hbm] * 6,
-        out_specs=hbm,
+        out_specs=pl.BlockSpec(memory_space=pltpu.VMEM),
         scratch_shapes=(
-            [pltpu.VMEM((span, block, wide), BF16)] * CHUNKS
-            + [pltpu.VMEM((n, cap, wide), BF16)] * CHUNKS
-            + [pltpu.VMEM((n, cap, wide), BF16)] * CHUNKS
-            + [pltpu.VMEM((seg_dev, wide), BF16)] * CHUNKS
+            [pltpu.VMEM((span, block, wide), BF16) for wide in wides]
+            + [pltpu.VMEM((n, cap, wide), BF16) for wide in wides]
+            + [pltpu.VMEM((n, cap, wide), BF16) for wide in wides]
+            + [pltpu.VMEM((max(RELAYED, default=1), 2, cap, wide), BF16) for wide in wides]
             + [
                 pltpu.SMEM(block_cols.shape, jnp.int32),
                 pltpu.VMEM((1, count), jnp.int32),
@@ -286,7 +344,8 @@
                 dma((CHUNKS + 1,)),
                 dma((CHUNKS,)),
                 dma((CHUNKS,)),
-                dma((CHUNKS,)),
+                dma((CHUNKS, max(RELAYED, default=1))),
+                dma((CHUNKS, max(RELAYED, default=1))),
                 dma((2,)),
                 dma((4, CHUNKS)),
                 dma((4, CHUNKS)),
@@ -294,14 +353,19 @@
             ]
         ),
         compiler_params=pltpu.CompilerParams(
-            collective_id=0, has_side_effects=True, vmem_limit_bytes=60 * 2**20
+            collective_id=0, has_side_effects=True, vmem_limit_bytes=48 * 2**20
         ),
         cost_estimate=pl.CostEstimate(
             flops=2 * rows_dev * stored * block * block * width,
             bytes_accessed=2 * (inductance.size + 2 * base_currents.size + term_rows.size),
             transcendentals=0,
         ),
-    )(block_cols, term_owner.reshape(1, count), term_slot.reshape(1, count), term_rows, base_currents, inductance)
+    )(*[
+        pltpu.with_memory_space_constraint(array, pltpu.HBM)
+        for array in (
+            block_cols, term_owner.reshape(1, count), term_slot.reshape(1, count), term_rows, base_currents, inductance
+        )
+    ])
 
 
 def solution(mesh):

time: 83.1 us -> 79 us (0.951)
  Pallas kernels: 79.1 us -> 77.1 us
  local copies, waits for them, and re-layouts: 3.08 us -> 1.32 us
    pallas_call x1, Pallas kernels: 79.1 us -> 77.1 us  [shards(): pl.pallas_call(functools.partial(kernel, n, cap), out_shape=pltpu.VMEM((s...]
    unnamed x1, local copies, waits for them, and re-layouts: 3.08 us -> 1.32 us
where the time goes in v1:
time: 79 us; the launch traced here: 78.4 us
  Pallas kernels  77.1 us (98%)
  local copies, waits for them, and re-layouts  1.32 us (2%)
    pallas_call x1, Pallas kernels, shards(): pl.pallas_call(functools.partial(kernel, n, cap), out_shape=pltpu.VMEM((s...  77.1 us

profile of v1, /device:TPU:5, one launch (start us, length us, event | category | flops | bytes accessed | tf_op | source)
XLA Modules:
  0.0 78.4 jit_solution(11146328440188970705)
XLA Ops:
  0.0 77.1 %shard_map.64 = bf16[1024,1024]{1,0:T(8,128)(2,1)S(1)} custom-call(s32[4,20]{1,0:T(4,128)} %cols_hbm.1, s32[1,256]{1,0:T(1,128)} %bitcast.2, s32[1,256]{1,0:T(1,128)} %bitcast.3, bf16[256,1024]{1,0:T(8,128)(2,1)} %terms_hbm.1, bf16[1024,1024]{1,0:T(8,128)(2,1)} %base_hbm.1, bf16[4,20,256,256]{3,2,1,0:T(8,128)(2,1)} %blocks_hbm.1), custom_call_target="tpu_custom_call" | custom-call | flops 10737418240 | bytes 15204352 | tf_op jit(solution)/shard_map/pallas_call | solution.py:323
  77.1 1.3 %copy.8 = bf16[1024,1024]{1,0:T(8,128)(2,1)} copy(bf16[1024,1024]{1,0:T(8,128)(2,1)S(1)} %shard_map.64) | data formatting | bytes 4194304

commit v2 on v1

--- a/solution.py
+++ b/solution.py
@@ -15,8 +15,12 @@
 F32 = jnp.float32
 BF16 = jnp.bfloat16
 TO_Y, TO_Z, TO_CORE, TO_RELAY = range(4)
-RELAYED = (1, 2)
-AHEAD = 2
+RELAYED = ((), (), (1, 2), (1, 2), (1, 2))
+DEPTH = 4
+EARLY = 0
+EDGE = False
+LAGS = (5, 5, 6, 6)
+SENDS = ((0,), (1, 2), (3,), (4,))
 
 
 def kernel(n, cap, cols_hbm, owner_hbm, slot_hbm, terms_hbm, base_hbm, blocks_hbm, out_ref, *scratch):
@@ -116,16 +120,20 @@
             src_ref=passing[j].at[hop - 1], dst_ref=passing[j].at[hop - 1], send_sem=pass_send.at[j, hop - 1],
             recv_sem=pass_recv.at[j, hop - 1], device_id={"row": y_peer}, device_id_type=MESH)
 
+    def plane(there):
+        return jnp.logical_and(there >= 0, there < n // 4)
+
+    def straight(hop, behind):
+        return jnp.logical_and(EDGE and hop == 2, jnp.logical_and(me % 2 == 1, jnp.logical_not(plane(behind))))
+
     def goes_over(hop):
-        there = my_z + hop * sign_y
-        return jnp.logical_and(there >= 0, there < n // 4)
+        return jnp.logical_and(plane(my_z + hop * sign_y), jnp.logical_not(straight(hop, my_z - sign_y)))
 
     def comes_over(hop):
-        there = my_z - hop * sign_y
-        return jnp.logical_and(there >= 0, there < n // 4)
+        return jnp.logical_and(plane(my_z - hop * sign_y), jnp.logical_not(straight(hop, my_z + sign_y)))
 
     def pass_rows(j):
-        for hop in RELAYED:
+        for hop in RELAYED[j]:
             @pl.when(comes_over(hop))
             def _(hop=hop):
                 passed(j, hop).wait_recv()
@@ -133,7 +141,7 @@
                     over_z(j, hop, core).start()
 
     def send_over(j):
-        for hop in reversed(RELAYED):
+        for hop in reversed(RELAYED[j]):
             @pl.when(goes_over(hop))
             def _(hop=hop):
                 over_y(j, hop).start()
@@ -144,7 +152,10 @@
             peer = (me + step) % n
             hops = (peer // 4 - my_z) * sign_y
             other_y = (peer // 2) % 2 != (me // 2) % 2
-            over = jnp.logical_and(other_y, jnp.logical_and(hops >= min(RELAYED, default=n), hops <= max(RELAYED, default=0)))
+            over = jnp.bool_(False)
+            for hop in RELAYED[j]:
+                over = jnp.logical_or(over, jnp.logical_and(hops == hop, goes_over(hop)))
+            over = jnp.logical_and(other_y, over)
 
             @pl.when(jnp.logical_not(over))
             def _():
@@ -170,17 +181,20 @@
         tags_out[peer] = jnp.broadcast_to(tags[peer:peer + 1], tags_out.shape[1:])
 
     pl.semaphore_wait(barrier, n - 1)
-    send_over(0)
-    send_rows(0)
+    for j in SENDS[0]:
+        send_over(j)
+        send_rows(j)
 
     @pl.loop(1, n)
     def _(step):
         tag_copy((me + step) % n, me).start()
 
     own_tags.start()
-    pass_rows(0)
-    for j in range(1, CHUNKS):
-        send_over(j)
+    for j in SENDS[0]:
+        pass_rows(j)
+    for j in range(CHUNKS):
+        if j not in SENDS[0]:
+            send_over(j)
 
     all_tags().wait_recv()
     own_tags.wait()
@@ -223,16 +237,15 @@
     def own(j):
         all_rows(j).wait_recv()
         own_rows[j].wait()
-        if j + 1 < CHUNKS:
-            send_rows(j + 1)
-            pass_rows(j + 1)
+        for i in SENDS[j + 1] if j + 1 < len(SENDS) else ():
+            send_rows(i)
+            pass_rows(i)
         rows = arrived[j][...].reshape(n * cap, wides[j])
         for q in range(rows_dev):
             place = slice(q * block, (q + 1) * block)
             injected = jnp.dot(landing[place], rows, preferred_element_type=F32)
             before_it = base[place, starts[j]:starts[j] + wides[j]].astype(F32)
             windows[j][HALO * rows_dev + q] = (before_it + injected).astype(BF16)
-            piece_copy(TO_Y, j * rows_dev + q, *y_way).start()
         halo_copy(TO_CORE, j, *core_way).start()
 
     def y_arrives(p):
@@ -273,22 +286,36 @@
         out_ref[r * block:(r + 1) * block, starts[j]:starts[j] + wides[j]] = total.astype(BF16)
 
     own(0)
-    z_lag, lag = 2, rows_dev + 2
-    for p in range(pieces + lag):
+    for p in range(DEPTH):
+        if p > 0 and p % rows_dev == 0:
+            own(p // rows_dev)
+        piece_copy(TO_Y, p, *y_way).start()
+    for p in range(DEPTH, DEPTH + EARLY):
+        if p % rows_dev == 0:
+            own(p // rows_dev)
+    z_lag = 2
+    first_compute = min(LAGS)
+    for p in range(pieces - rows_dev + max(LAGS) + 1):
         if p < pieces:
             y_arrives(p)
-            if p % rows_dev == rows_dev - 1 - AHEAD and p // rows_dev + 1 < CHUNKS:
-                own(p // rows_dev + 1)
+            if p + DEPTH < pieces:
+                if (p + DEPTH) // rows_dev > 0 and (p + DEPTH) % rows_dev == 0 and not EARLY:
+                    own((p + DEPTH) // rows_dev)
+                piece_copy(TO_Y, p + DEPTH, *y_way).start()
+            ready = p + DEPTH + EARLY
+            if EARLY and ready % rows_dev == 0 and 0 < ready // rows_dev < CHUNKS:
+                own(ready // rows_dev)
         if 0 <= p - z_lag < pieces:
             z_arrives(p - z_lag)
-        if p == lag:
+        if p == first_compute:
             load_cols.wait()
             load_blocks.wait()
-        if p >= lag:
-            j, r = divmod(p - lag, rows_dev)
-            if r == 0:
-                window_complete(j)
-            compute(j, r)
+        for j in range(CHUNKS):
+            for r in range(rows_dev):
+                if p == rows_dev * j + LAGS[r % len(LAGS)]:
+                    if r == 0:
+                        window_complete(j)
+                    compute(j, r)
 
     all_tags().wait_send()
     for j in range(CHUNKS):
@@ -304,7 +331,7 @@
         def _():
             halo_copy(TO_RELAY, j, *relay_way).wait_send()
 
-        for hop in RELAYED:
+        for hop in RELAYED[j]:
             @pl.when(comes_over(hop))
             def _(hop=hop):
                 passed(j, hop).wait_send()
@@ -329,7 +356,7 @@
             [pltpu.VMEM((span, block, wide), BF16) for wide in wides]
             + [pltpu.VMEM((n, cap, wide), BF16) for wide in wides]
             + [pltpu.VMEM((n, cap, wide), BF16) for wide in wides]
-            + [pltpu.VMEM((max(RELAYED, default=1), 2, cap, wide), BF16) for wide in wides]
+            + [pltpu.VMEM((2, 2, cap, wide), BF16) for wide in wides]
             + [
                 pltpu.SMEM(block_cols.shape, jnp.int32),
                 pltpu.VMEM((1, count), jnp.int32),
@@ -344,8 +371,8 @@
                 dma((CHUNKS + 1,)),
                 dma((CHUNKS,)),
                 dma((CHUNKS,)),
-                dma((CHUNKS, max(RELAYED, default=1))),
-                dma((CHUNKS, max(RELAYED, default=1))),
+                dma((CHUNKS, 2)),
+                dma((CHUNKS, 2)),
                 dma((2,)),
                 dma((4, CHUNKS)),
                 dma((4, CHUNKS)),

time: 79 us -> 77.2 us (0.977)
  Pallas kernels: 77.1 us -> 75.7 us
    pallas_call x1, Pallas kernels: 77.1 us -> 75.7 us  [shards(): pl.pallas_call(functools.partial(kernel, n, cap), out_shape=pltpu.VMEM((s...]
where the time goes in v2:
time: 77.2 us; the launch traced here: 77 us
  Pallas kernels  75.7 us (98%)
  local copies, waits for them, and re-layouts  1.32 us (2%)
    pallas_call x1, Pallas kernels, shards(): pl.pallas_call(functools.partial(kernel, n, cap), out_shape=pltpu.VMEM((s...  75.7 us

profile of v2, /device:TPU:5, one launch (start us, length us, event | category | flops | bytes accessed | tf_op | source)
XLA Modules:
  0.0 77.0 jit_solution(2576777965564893255)
XLA Ops:
  0.0 75.7 %shard_map.64 = bf16[1024,1024]{1,0:T(8,128)(2,1)S(1)} custom-call(s32[4,20]{1,0:T(4,128)} %cols_hbm.1, s32[1,256]{1,0:T(1,128)} %bitcast.2, s32[1,256]{1,0:T(1,128)} %bitcast.3, bf16[256,1024]{1,0:T(8,128)(2,1)} %terms_hbm.1, bf16[1024,1024]{1,0:T(8,128)(2,1)} %base_hbm.1, bf16[4,20,256,256]{3,2,1,0:T(8,128)(2,1)} %blocks_hbm.1), custom_call_target="tpu_custom_call" | custom-call | flops 10737418240 | bytes 15204352 | tf_op jit(solution)/shard_map/pallas_call | solution.py:350
  75.7 1.3 %copy.8 = bf16[1024,1024]{1,0:T(8,128)(2,1)} copy(bf16[1024,1024]{1,0:T(8,128)(2,1)S(1)} %shard_map.64) | data formatting | bytes 4194304

commit v3 on v2

--- a/solution.py
+++ b/solution.py
@@ -16,11 +16,11 @@
 BF16 = jnp.bfloat16
 TO_Y, TO_Z, TO_CORE, TO_RELAY = range(4)
 RELAYED = ((), (), (1, 2), (1, 2), (1, 2))
-DEPTH = 4
-EARLY = 0
+DEPTHS = (4, 4, 4, 4, 4)
+Z_LAG = 2
 EDGE = False
 LAGS = (5, 5, 6, 6)
-SENDS = ((0,), (1, 2), (3,), (4,))
+SENDS = ((0,), (1, 2), (), (3,), (4,))
 
 
 def kernel(n, cap, cols_hbm, owner_hbm, slot_hbm, terms_hbm, base_hbm, blocks_hbm, out_ref, *scratch):
@@ -181,21 +181,21 @@
         tags_out[peer] = jnp.broadcast_to(tags[peer:peer + 1], tags_out.shape[1:])
 
     pl.semaphore_wait(barrier, n - 1)
+
+    @pl.loop(1, n)
+    def _(step):
+        tag_copy((me + step) % n, me).start()
+
+    own_tags.start()
+
     for j in SENDS[0]:
         send_over(j)
         send_rows(j)
-
-    @pl.loop(1, n)
-    def _(step):
-        tag_copy((me + step) % n, me).start()
-
-    own_tags.start()
     for j in SENDS[0]:
         pass_rows(j)
     for j in range(CHUNKS):
         if j not in SENDS[0]:
             send_over(j)
-
     all_tags().wait_recv()
     own_tags.wait()
     packed = []
@@ -286,25 +286,19 @@
         out_ref[r * block:(r + 1) * block, starts[j]:starts[j] + wides[j]] = total.astype(BF16)
 
     own(0)
-    for p in range(DEPTH):
-        if p > 0 and p % rows_dev == 0:
-            own(p // rows_dev)
+    for p in range(rows_dev):
         piece_copy(TO_Y, p, *y_way).start()
-    for p in range(DEPTH, DEPTH + EARLY):
-        if p % rows_dev == 0:
-            own(p // rows_dev)
-    z_lag = 2
+    upcoming = rows_dev
+    z_lag = Z_LAG
     first_compute = min(LAGS)
     for p in range(pieces - rows_dev + max(LAGS) + 1):
         if p < pieces:
             y_arrives(p)
-            if p + DEPTH < pieces:
-                if (p + DEPTH) // rows_dev > 0 and (p + DEPTH) % rows_dev == 0 and not EARLY:
-                    own((p + DEPTH) // rows_dev)
-                piece_copy(TO_Y, p + DEPTH, *y_way).start()
-            ready = p + DEPTH + EARLY
-            if EARLY and ready % rows_dev == 0 and 0 < ready // rows_dev < CHUNKS:
-                own(ready // rows_dev)
+            while upcoming < pieces and upcoming - p <= DEPTHS[upcoming // rows_dev]:
+                if upcoming % rows_dev == 0:
+                    own(upcoming // rows_dev)
+                piece_copy(TO_Y, upcoming, *y_way).start()
+                upcoming += 1
         if 0 <= p - z_lag < pieces:
             z_arrives(p - z_lag)
         if p == first_compute:

time: 77.2 us -> 76.9 us (level)
  no operation moved by 1% of the time
where the time goes in v3:
time: 76.9 us; the launch traced here: 76.8 us
  Pallas kernels  75.4 us (98%)
  local copies, waits for them, and re-layouts  1.32 us (2%)
    pallas_call x1, Pallas kernels, shards(): pl.pallas_call(functools.partial(kernel, n, cap), out_shape=pltpu.VMEM((s...  75.4 us

profile of v3, /device:TPU:5, one launch (start us, length us, event | category | flops | bytes accessed | tf_op | source)
XLA Modules:
  0.0 76.8 jit_solution(9485358891833947455)
XLA Ops:
  0.0 75.4 %shard_map.64 = bf16[1024,1024]{1,0:T(8,128)(2,1)S(1)} custom-call(s32[4,20]{1,0:T(4,128)} %cols_hbm.1, s32[1,256]{1,0:T(1,128)} %bitcast.2, s32[1,256]{1,0:T(1,128)} %bitcast.3, bf16[256,1024]{1,0:T(8,128)(2,1)} %terms_hbm.1, bf16[1024,1024]{1,0:T(8,128)(2,1)} %base_hbm.1, bf16[4,20,256,256]{3,2,1,0:T(8,128)(2,1)} %blocks_hbm.1), custom_call_target="tpu_custom_call" | custom-call | flops 10737418240 | bytes 15204352 | tf_op jit(solution)/shard_map/pallas_call | solution.py:344
  75.4 1.3 %copy.8 = bf16[1024,1024]{1,0:T(8,128)(2,1)} copy(bf16[1024,1024]{1,0:T(8,128)(2,1)S(1)} %shard_map.64) | data formatting | bytes 4194304
